TPU v7x, 128 devices: a whole 4x4x4 slice. The times are simulated.
128 devices in a mesh: dp: 16 (over x_hi, z, core), seq: 8 (over y, x_lo).
Axes of the slice: x: 4 (x_hi: 2, x_lo: 2; x = x_hi * 2 + x_lo), y: 4, z: 4, core: 2. Of those that a mesh axis runs over, the one named last changes fastest.
Arguments:
- queries: bfloat16 [16384, 8192], P(('seq', 'dp')), may hold values from -4.5 to 4.5
- key_head_rows: bfloat16 [16384, 1024], P(('seq', 'dp')), may hold values from -4.5 to 4.5
- value_head_rows: bfloat16 [16384, 1024], P(('seq', 'dp')), may hold values from -6 to 6
- out_cotangent: bfloat16 [16384, 8192], P(('seq', 'dp')), may hold values from -6 to 6
- value_readout: bfloat16 [8192], replicated, may hold values from -0.29882812 to 0.29882812
- rewards: float32 [16384], P(('seq', 'dp')), may hold values from -1.5 to 1.5
- saved_values: float32 [16384], P(('seq', 'dp')), may hold values from -6 to 6
- episode_ends: int32 [16384], P(('seq', 'dp')), may hold values from 0 to 1, as said below
- segment_ids: int32 [16384], P(('seq', 'dp')), may hold values from 0 to 16, as said below
Outputs:
- query_grad: bfloat16 [16384, 8192], P(('seq', 'dp'))
- key_gradient: bfloat16 [16384, 1024], P(('seq', 'dp'))
- value_gradient: bfloat16 [16384, 1024], P(('seq', 'dp'))
- advantages: float32 [16384], P(('seq', 'dp'))
Inputs may be any that keep to these rules, and one draw needn't show every extreme that they name: `episode_ends`: 1 marks the last token of an episode; each aligned block of 1024 tokens holds exactly one 1, never at the block's last token. `segment_ids`: the number of episode ends before the token in the whole array; it never falls and rises by one right after each end.
All inputs are finite; a program needn't handle non-finite values.
Results may differ from a plain program's by a relative error of at most 0.0059.
Values may be sent and summed in bfloat16 or wider, within the bound.
A program may use at most 192 MiB of HBM per device.

v0:
```python
import math

import jax
import jax.numpy as jnp
from jax import lax
from jax.sharding import PartitionSpec as P

QUERY_HEADS = 64
KEY_VALUE_HEADS = 8
HEAD_WIDTH = 128


def from_behind(block, axis, distance):
    devices = range(lax.axis_size(axis))
    route = [(i - distance, i) for i in devices if i - distance in devices]
    return lax.ppermute(block, axis, route)


def head_probs(query_rows, key_rows, allowed):
    score_scale = 1.0 / math.sqrt(query_rows.shape[1])
    scores = jnp.dot(query_rows, key_rows.T, preferred_element_type=jnp.float32) * score_scale
    scores = jnp.where(allowed, scores, -jnp.inf)
    row_max = jnp.max(scores, axis=1, keepdims=True)
    row_sum = jnp.sum(jnp.exp(scores - row_max), axis=1, keepdims=True)
    log_total = row_max + jnp.log(row_sum)
    return jnp.exp(scores - log_total)


def head_forward(query_head, key_head, value_head, allowed):
    window_row_block = query_head.shape[0]
    half_rows = window_row_block // 2
    pieces = []
    for block_index in range(2):
        row_start = block_index * half_rows
        row_end = row_start + half_rows
        weights = head_probs(
            query_head[row_start:row_end], key_head[:row_end], allowed[row_start:row_end, :row_end]
        )
        pieces.append(
            jnp.dot(
                weights.astype(jnp.bfloat16),
                value_head[:row_end],
                preferred_element_type=jnp.float32,
            )
        )
    return jnp.concatenate(pieces, axis=0)


def head_backward(query_head, key_head, value_head, grad_out, output_head, allowed):
    window_row_block = query_head.shape[0]
    half_rows = window_row_block // 2
    score_scale = 1.0 / math.sqrt(query_head.shape[1])
    query_parts = []
    key_total = jnp.zeros(key_head.shape, jnp.float32)
    value_total = jnp.zeros(value_head.shape, jnp.float32)
    for block_index in range(2):
        row_start = block_index * half_rows
        row_end = row_start + half_rows
        weights = head_probs(
            query_head[row_start:row_end], key_head[:row_end], allowed[row_start:row_end, :row_end]
        )
        weights_low = weights.astype(jnp.bfloat16)
        grad_rows = grad_out[row_start:row_end]
        grad_probs = jnp.dot(grad_rows, value_head[:row_end].T, preferred_element_type=jnp.float32)
        row_dot = jnp.sum(
            grad_rows.astype(jnp.float32) * output_head[row_start:row_end], axis=1, keepdims=True
        )
        grad_scores = (weights * (grad_probs - row_dot)).astype(jnp.bfloat16)
        query_parts.append(
            jnp.dot(grad_scores, key_head[:row_end], preferred_element_type=jnp.float32)
            * score_scale
        )
        key_part = (
            lax.dot_general(
                grad_scores,
                query_head[row_start:row_end],
                (((0,), (0,)), ((), ())),
                preferred_element_type=jnp.float32,
            )
            * score_scale
        )
        value_part = lax.dot_general(
            weights_low, grad_rows, (((0,), (0,)), ((), ())), preferred_element_type=jnp.float32
        )
        key_total = key_total + jnp.pad(key_part, ((0, window_row_block - row_end), (0, 0)))
        value_total = value_total + jnp.pad(value_part, ((0, window_row_block - row_end), (0, 0)))
    return (jnp.concatenate(query_parts, axis=0), key_total, value_total)


def compose(earlier, later):
    return (later[0] * earlier[0], later[1] + later[0] * earlier[1])


def suffix_from(factors, offsets, lowest):
    length = factors.shape[0]

    def fold_element(folded, element):
        position, factor, offset = element
        joined = compose(folded, (factor, offset))
        chosen = position >= lowest
        return (
            (jnp.where(chosen, joined[0], folded[0]), jnp.where(chosen, joined[1], folded[1])),
            None,
        )

    initial = (jnp.ones((), jnp.float32), jnp.zeros((), jnp.float32))
    result, _ = lax.scan(
        fold_element, initial, (jnp.arange(length), factors, offsets), reverse=True
    )
    return result


def local_returns(rewards, episode_ends):
    length = rewards.shape[0]
    before = jnp.cumsum(episode_ends) - episode_ends
    position = jnp.arange(length)
    reaching = (position[None, :] >= position[:, None]) & (before[None, :] == before[:, None])
    local_gain = jnp.dot(reaching.astype(jnp.float32), rewards, precision=lax.Precision.HIGHEST)
    remaining = jnp.sum(episode_ends) - before
    passing = (remaining == 0).astype(jnp.float32)
    return (local_gain, passing)


def body(
    queries,
    key_head_rows,
    value_head_rows,
    out_cotangent,
    value_readout,
    rewards,
    saved_values,
    episode_ends,
    segment_ids,
):
    replica_count = lax.axis_size("dp")
    seq_count = lax.axis_size("seq")
    dp_place = lax.axis_index("dp")
    seq_place = lax.axis_index("seq")
    token_rows = rewards.shape[0]
    shard_place = seq_place * replica_count + dp_place
    rollout_end = (shard_place == replica_count * seq_count // 2 - 1).astype(jnp.float32)
    local_gain, passing = local_returns(rewards, episode_ends)
    through = (jnp.sum(episode_ends) == 0).astype(jnp.float32) * (1.0 - rollout_end)
    factor = jnp.reshape(through, (1,))
    offset = local_gain[:1]
    group_factors, group_offsets = (
        lax.all_gather(factor, "dp", axis=0, tiled=True),
        lax.all_gather(offset, "dp", axis=0, tiled=True),
    )
    inside = suffix_from(group_factors, group_offsets, dp_place + 1)
    group_total = suffix_from(group_factors, group_offsets, 0)
    beyond = from_behind(group_total[1].reshape(1), "seq", -1)
    entering = inside[1] + inside[0] * beyond[0]
    entering = entering * (1.0 - rollout_end)
    gains = local_gain + passing * entering
    advantages = gains - saved_values
    local_heads = QUERY_HEADS // replica_count
    repeat_factor = replica_count // KEY_VALUE_HEADS
    key_wide = jnp.broadcast_to(
        key_head_rows.reshape(token_rows, KEY_VALUE_HEADS, 1, HEAD_WIDTH),
        (token_rows, KEY_VALUE_HEADS, repeat_factor, HEAD_WIDTH),
    ).reshape(token_rows, replica_count * HEAD_WIDTH)
    value_wide = jnp.broadcast_to(
        value_head_rows.reshape(token_rows, KEY_VALUE_HEADS, 1, HEAD_WIDTH),
        (token_rows, KEY_VALUE_HEADS, repeat_factor, HEAD_WIDTH),
    ).reshape(token_rows, replica_count * HEAD_WIDTH)
    window_segs = lax.all_gather(segment_ids, "dp", axis=0, tiled=True)
    head_queries, head_keys, head_values, head_cotan = (
        lax.all_to_all(queries, "dp", split_axis=1, concat_axis=0, tiled=True),
        lax.all_to_all(key_wide, "dp", split_axis=1, concat_axis=0, tiled=True),
        lax.all_to_all(value_wide, "dp", split_axis=1, concat_axis=0, tiled=True),
        lax.all_to_all(out_cotangent, "dp", split_axis=1, concat_axis=0, tiled=True),
    )
    window_row_block = head_queries.shape[0]
    position = jnp.arange(window_row_block)
    allowed = (position[None, :] <= position[:, None]) & (
        window_segs[None, :] == window_segs[:, None]
    )
    readout = lax.dynamic_slice_in_dim(
        value_readout, dp_place * local_heads * HEAD_WIDTH, local_heads * HEAD_WIDTH, 0
    ).astype(jnp.float32)
    outputs = []
    estimate = jnp.zeros((window_row_block,), jnp.float32)
    for h in range(local_heads):
        output_head = head_forward(
            head_queries[:, h * HEAD_WIDTH : (h + 1) * HEAD_WIDTH], head_keys, head_values, allowed
        )
        outputs.append(output_head)
        estimate = estimate + jnp.dot(
            output_head,
            readout[h * HEAD_WIDTH : (h + 1) * HEAD_WIDTH],
            precision=lax.Precision.HIGHEST,
        )
    placed = lax.dynamic_update_slice_in_dim(
        jnp.zeros((window_row_block,), jnp.float32), gains, dp_place * token_rows, 0
    )
    value_error = lax.psum(estimate - placed, "dp")
    query_pieces = []
    key_total = jnp.zeros((window_row_block, HEAD_WIDTH), jnp.float32)
    value_total = jnp.zeros((window_row_block, HEAD_WIDTH), jnp.float32)
    for h in range(local_heads):
        columns = slice(h * HEAD_WIDTH, (h + 1) * HEAD_WIDTH)
        grad_out = (
            head_cotan[:, columns].astype(jnp.float32)
            + value_error[:, None] * readout[None, columns]
        ).astype(jnp.bfloat16)
        query_part, key_part, value_part = head_backward(
            head_queries[:, columns], head_keys, head_values, grad_out, outputs[h], allowed
        )
        query_pieces.append(query_part.astype(jnp.bfloat16))
        key_total = key_total + key_part
        value_total = value_total + value_part
    grad_query_heads = jnp.concatenate(query_pieces, axis=1)
    query_grad = lax.all_to_all(grad_query_heads, "dp", split_axis=0, concat_axis=1, tiled=True)
    key_expanded, value_expanded = (
        lax.all_to_all(key_total, "dp", split_axis=0, concat_axis=1, tiled=True),
        lax.all_to_all(value_total, "dp", split_axis=0, concat_axis=1, tiled=True),
    )
    key_gradient = (
        key_expanded.reshape(token_rows, KEY_VALUE_HEADS, repeat_factor, HEAD_WIDTH)
        .sum(axis=2)
        .astype(jnp.bfloat16)
        .reshape(token_rows, KEY_VALUE_HEADS * HEAD_WIDTH)
    )
    value_gradient = (
        value_expanded.reshape(token_rows, KEY_VALUE_HEADS, repeat_factor, HEAD_WIDTH)
        .sum(axis=2)
        .astype(jnp.bfloat16)
        .reshape(token_rows, KEY_VALUE_HEADS * HEAD_WIDTH)
    )
    return (query_grad, key_gradient, value_gradient, advantages)


def solution(mesh):
    in_specs = (
        P(("seq", "dp"), None),
        P(("seq", "dp"), None),
        P(("seq", "dp"), None),
        P(("seq", "dp"), None),
        P(),
        P(("seq", "dp")),
        P(("seq", "dp")),
        P(("seq", "dp")),
        P(("seq", "dp")),
    )
    out_specs = (
        P(("seq", "dp"), None),
        P(("seq", "dp"), None),
        P(("seq", "dp"), None),
        P(("seq", "dp")),
    )
    return jax.shard_map(body, mesh=mesh, in_specs=in_specs, out_specs=out_specs, check_vma=False)
```

profile of v0, /device:TPU:24, one launch (start us, length us, event | category | flops | bytes accessed | tf_op | source)
XLA Modules:
  0.0 494.9 jit_solution(2843104927148625701)
XLA Ops:
  2.5 7.9 %all-to-all-start.1 = ((bf16[128,16,128]{2,0,1:T(8,128)(2,1)}), bf16[128,16,128]{2,0,1:T(8,128)(2,1)S(1)}, u32[]{:S(2)}, u32[]{:S(2)}) async-start(bf16[128,16,128]{2,0,1:T(8,128)(2,1)} %bitcast.11), calls=%async_computation.1 | async-start | bytes 1048576 | tf_op jit(solution)/shard_map/all_to_all | solution.py:170
  11.4 11.4 %all-to-all-done.1 = bf16[128,16,128]{2,0,1:T(8,128)(2,1)S(1)} async-done(((bf16[128,16,128]{2,0,1:T(8,128)(2,1)}), bf16[128,16,128]{2,0,1:T(8,128)(2,1)S(1)}, u32[]{:S(2)}, u32[]{:S(2)}) %all-to-all-start.1) | async-done | bytes 524320 | tf_op jit(solution)/shard_map/all_to_all | solution.py:170
  23.8 3.6 all-to-all-start.3
  27.4 4.1 copy.83
  31.9 7.8 %all-to-all-done.3 = bf16[128,16,128]{2,0,1:T(8,128)(2,1)S(1)} async-done(((bf16[128,16,128]{2,0,1:T(8,128)(2,1)}), bf16[128,16,128]{2,0,1:T(8,128)(2,1)S(1)}, u32[]{:S(2)}, u32[]{:S(2)}) %all-to-all-start.3) | async-done | bytes 524320 | tf_op jit(solution)/shard_map/all_to_all | solution.py:171
  39.7 4.6 all-to-all-start
  47.9 51.3 %all-reduce.10 = (f32[16]{0:T(128)S(1)}, f32[16]{0:T(128)S(1)}) all-reduce(f32[16]{0:T(128)S(1)} %dynamic-update-slice, f32[16]{0:T(128)S(1)} %slice_dynamic-update-slice_fusion), channel_id=1, replica_groups=mesh['dp'=16,'seq'=8] {'dp'}, use_global_device_ids=true, to_apply=%add.8 | all-reduce | flops 32 | bytes 256
  99.2 58.9 %while.31 = (s32[]{:T(128)}, f32[]{:T(128)}, s32[16]{0:T(128)S(1)}, f32[16]{0:T(128)S(1)}, f32[16]{0:T(128)S(1)}, /*index=5*/s32[]{:T(128)}, s32[]{:T(128)}, s32[1]{0:T(128)}) while((s32[]{:T(128)}, f32[]{:T(128)}, s32[16]{0:T(128)S(1)}, f32[16]{0:T(128)S(1)}, f32[16]{0:T(128)S(1)}, /*index=5*/s32[]{:T(128)}, s32[]{:T(128)}, ...), condition=%wide.region_21.22_spmd, body=%wide.region_20.21_spmd.sunk | while | flops 7 | bytes 179 | solution.py:107
  158.2 3.6 collective-permute-start
  161.8 3.2 copy.125
  165.7 18.8 %all-gather = s32[16,1,128]{2,1,0:T(1,128)S(1)} all-gather(s32[1,1,128]{2,1,0:T(1,128)S(1)} %bitcast.223), channel_id=1, replica_groups=mesh['dp'=16,'seq'=8] {'dp'}, dimensions={0}, use_global_device_ids=true | all-gather | bytes 8704 | tf_op jit(solution)/shard_map/all_gather | solution.py:167
  184.5 67.7 %while.30 = (s32[]{:T(128)}, f32[]{:T(128)}, f32[]{:T(128)}, s32[16]{0:T(128)S(1)}, s32[]{:T(128)}, /*index=5*/f32[16]{0:T(128)S(1)}, f32[16]{0:T(128)S(1)}, s32[]{:T(128)}, s32[]{:T(128)}) while((s32[]{:T(128)}, f32[]{:T(128)}, f32[]{:T(128)}, s32[16]{0:T(128)S(1)}, s32[]{:T(128)}, /*index=5*/f32[16]{0:T(128)S(1)}, f32[16]{0:T(128)S(1)}, ...), condition=%wide.region_19.20_spmd, body=%wide.region_18.19_spmd.sunk | while | flops 9 | bytes 212 | solution.py:107
  252.3 5.4 %fusion = pred[2048,2048]{0,1:T(32,128)(4,1)} fusion(s32[2048]{0:T(1024)S(1)} %bitcast.217), kind=kLoop, calls=%fused_computation.1 | loop fusion | flops 12582912 | bytes 4202496 | tf_op jit(solution)/shard_map/and | solution.py:176
  259.8 8.1 %all-to-all-start.2 = ((bf16[128,16,512]{2,0,1:T(8,128)(2,1)}), bf16[128,16,512]{2,0,1:T(8,128)(2,1)}, u32[]{:S(2)}, u32[]{:S(2)}) async-start(bf16[128,16,512]{2,0,1:T(8,128)(2,1)} %bitcast.173), calls=%async_computation.2 | async-start | bytes 4194304 | tf_op jit(solution)/shard_map/all_to_all | solution.py:172
  267.9 3.9 copy.84
  271.8 2.3 fusion.133
  275.0 3.3 fusion.131
  278.3 2.5 fusion.132
  280.8 5.7 %fusion.130 = (f32[1024]{0:T(1024)S(1)}, f32[1024,2048]{0,1:T(8,128)}) fusion(bf16[2048,128]{1,0:T(8,128)(2,1)S(1)} %bitcast.200, bf16[2048,512]{1,0:T(8,128)(2,1)S(1)} %bitcast.178, pred[2048,2048]{0,1:T(32,128)(4,1)S(1)} %copy-done.32), kind=kOutput, calls=%fused_computation.200 | convolution fusion | flops 543161344 | bytes 11276288 | tf_op jit(solution)/shard_map/dot_general | solution.py:21
  286.6 3.1 fusion.129
  289.6 2.5 fusion.128
  292.1 3.0 fusion.127
  295.2 3.6 fusion.126
  300.6 1.5 copy-done.11
  304.3 4.7 exponential_reduce_fusion.3
  309.1 1.3 fusion.34
  310.4 4.9 fusion.37
  318.0 1.5 fusion.31
  324.0 1.3 fusion.28
  326.7 39.3 %psum.7 = f32[2048]{0:T(1024)S(1)} all-reduce(f32[2048]{0:T(1024)S(1)} %add_subtract_fusion), channel_id=1, replica_groups=mesh['dp'=16,'seq'=8] {'dp'}, use_global_device_ids=true, to_apply=%region_22.23 | all-reduce | flops 2048 | bytes 16384 | tf_op jit(solution)/shard_map/psum | solution.py:197
  366.0 2.3 add_convert_fusion.3
  376.4 1.5 convolution_multiply_fusion.11
  377.9 1.5 fusion.19
  380.3 1.5 convolution_multiply_fusion.10
  381.8 1.5 fusion.20
  384.2 1.6 convolution_multiply_fusion.9
  386.6 1.3 multiply_convert_fusion.4
  387.9 1.5 convolution_multiply_fusion.8
  390.3 1.5 convolution_add_fusion.3
  391.8 1.5 slice-done.5
  393.3 1.5 fusion.11
  394.8 1.5 fusion.10
  397.2 2.5 fusion.9
  399.7 4.5 all-to-all-start.6
  404.2 5.1 %multiply_convert_fusion.3 = bf16[1024,2048]{0,1:T(8,128)(2,1)S(1)} fusion(f32[1024,2048]{0,1:T(8,128)} %get-tuple-element.311, bf16[2048,128]{1,0:T(8,128)(2,1)S(1)} %bitcast.160, f32[1024]{0:T(1024)S(1)} %get-tuple-element.318, f32[1024]{0:T(1024)S(1)} %log_add_fusion.6, bf16[2048,128]{1,0:T(8,128)(2,1)S(1)} %get-tuple-element.292), kind=kOutput, calls=%fused_computation.5 | convolution fusion | flops 545259520 | bytes 13377536 | tf_op jit(solution)/shard_map/dot_general | solution.py:64
  409.4 1.3 fusion.23
  412.3 5.2 %multiply_convert_fusion.2 = bf16[1024,2048]{0,1:T(8,128)(2,1)S(1)} fusion(f32[1024,2048]{0,1:T(8,128)} %copy-done.3, bf16[2048,128]{1,0:T(8,128)(2,1)S(1)} %bitcast.161, f32[1024]{0:T(1024)S(1)} %get-tuple-element.320, f32[1024]{0:T(1024)S(1)} %log_add_fusion.4, bf16[2048,128]{1,0:T(8,128)(2,1)S(1)} %get-tuple-element.295), kind=kOutput, calls=%fused_computation.4 | convolution fusion | flops 545259520 | bytes 13377536 | tf_op jit(solution)/shard_map/dot_general | solution.py:64
  417.6 1.8 multiply_convert_fusion.1
  419.3 1.3 fusion.24
  420.7 2.0 fusion.25
  422.7 1.3 fusion.17
  424.0 1.5 fusion.15
  426.7 3.7 multiply_convert_fusion
  430.4 4.5 fusion.13
  435.0 7.1 %all-to-all-start.5 = ((f32[16,128,128]{2,1,0:T(8,128)}), f32[16,128,128]{2,1,0:T(8,128)S(1)}, u32[]{:S(2)}, u32[]{:S(2)}) async-start(f32[16,128,128]{2,1,0:T(8,128)} %bitcast.44), calls=%async_computation.5 | async-start | bytes 2097152 | tf_op jit(solution)/shard_map/all_to_all | solution.py:216
  442.1 3.5 fusion.26
  445.7 1.6 pad_maximum_fusion
  447.3 12.7 %all-to-all-done.5 = f32[16,128,128]{2,1,0:T(8,128)S(1)} async-done(((f32[16,128,128]{2,1,0:T(8,128)}), f32[16,128,128]{2,1,0:T(8,128)S(1)}, u32[]{:S(2)}, u32[]{:S(2)}) %all-to-all-start.5) | async-done | bytes 1048608 | tf_op jit(solution)/shard_map/all_to_all | solution.py:216
  460.1 3.7 all-to-all-start.4
  463.8 2.1 bitcast_reduce_fusion
  465.9 1.8 copy.103
  467.7 1.8 copy.105
  472.3 20.8 %all-to-all-done.4 = bf16[16,128,512]{2,1,0:T(8,128)(2,1)S(1)} async-done(((bf16[16,128,512]{2,1,0:T(8,128)(2,1)}), bf16[16,128,512]{2,1,0:T(8,128)(2,1)S(1)}, u32[]{:S(2)}, u32[]{:S(2)}) %all-to-all-start.4) | async-done | bytes 2097184 | tf_op jit(solution)/shard_map/all_to_all | solution.py:214
  493.1 1.5 copy.121
  (292 shorter events, 98.4 us)
Async XLA Ops:
  1.6 29.8 %copy-start.44 = (s32[128]{0:T(128)S(1)}, s32[128]{0:T(128)}, u32[]{:S(2)}) copy-start(s32[128]{0:T(128)} %param.20) | copy-start | bytes 1540
  2.5 20.2 %all-to-all-start.1 = ((bf16[128,16,128]{2,0,1:T(8,128)(2,1)}), bf16[128,16,128]{2,0,1:T(8,128)(2,1)S(1)}, u32[]{:S(2)}, u32[]{:S(2)}) async-start(bf16[128,16,128]{2,0,1:T(8,128)(2,1)} %bitcast.11), calls=%async_computation.1 | async-start | bytes 1048576 | tf_op jit(solution)/shard_map/all_to_all | solution.py:170
  22.8 269.3 %copy-start.38 = (bf16[128,16,128]{2,0,1:T(8,128)(2,1)}, bf16[128,16,128]{2,0,1:T(8,128)(2,1)S(1)}, u32[]{:S(2)}) copy-start(bf16[128,16,128]{2,0,1:T(8,128)(2,1)S(1)} %all-to-all-done.1) | copy-start | bytes 1572868
  23.8 15.9 %all-to-all-start.3 = ((bf16[128,16,128]{2,0,1:T(8,128)(2,1)}), bf16[128,16,128]{2,0,1:T(8,128)(2,1)S(1)}, u32[]{:S(2)}, u32[]{:S(2)}) async-start(bf16[128,16,128]{2,0,1:T(8,128)(2,1)} %bitcast.16), calls=%async_computation.3 | async-start | bytes 1048576 | tf_op jit(solution)/shard_map/all_to_all | solution.py:171
  27.4 18.2 %copy-start.48 = (u32[128]{0:T(128)S(1)}, u32[128]{0:T(128)}, u32[]{:S(2)}) copy-start(u32[128]{0:T(128)} %constant.124) | copy-start | bytes 1540
  27.4 19.6 %copy-start.47 = (f32[128]{0:T(128)S(1)}, f32[128]{0:T(128)}, u32[]{:S(2)}) copy-start(f32[128]{0:T(128)} %param.18) | copy-start | bytes 1540
  39.7 126.0 %copy-start.45 = (s32[128]{0:T(128)S(1)}, s32[128]{0:T(128)}, u32[]{:S(2)}) copy-start(s32[128]{0:T(128)} %param.21) | copy-start | bytes 1540
  39.7 220.1 %all-to-all-start = ((bf16[128,16,512]{0,2,1:T(8,128)(2,1)}), bf16[128,16,512]{0,2,1:T(8,128)(2,1)}, u32[]{:S(2)}, u32[]{:S(2)}) async-start(bf16[128,16,512]{0,2,1:T(8,128)(2,1)} %bitcast.172), calls=%async_computation | async-start | bytes 4194304 | tf_op jit(solution)/shard_map/all_to_all | solution.py:169
  158.2 99.6 %collective-permute-start = (f32[1]{0:T(128)}, f32[1]{0:T(128)}, u32[]{:S(2)}, u32[]{:S(2)}) collective-permute-start(f32[1]{0:T(128)} %bitcast.36), channel_id=1, source_target_pairs={{1,0},{2,1},{3,2},{4,3},{5,4},{6,5},{7,6},{9,8},{10,9},{11,10},{12... | collective-permute-start | bytes 20 | tf_op jit(solution)/shard_map/ppermute | solution.py:16
  161.8 96.6 %copy-start.46 = (f32[128]{0:T(128)S(1)}, f32[128]{0:T(128)}, u32[]{:S(2)}) copy-start(f32[128]{0:T(128)} %param.19) | copy-start | bytes 1540
  259.8 106.2 %all-to-all-start.2 = ((bf16[128,16,512]{2,0,1:T(8,128)(2,1)}), bf16[128,16,512]{2,0,1:T(8,128)(2,1)}, u32[]{:S(2)}, u32[]{:S(2)}) async-start(bf16[128,16,512]{2,0,1:T(8,128)(2,1)} %bitcast.173), calls=%async_computation.2 | async-start | bytes 4194304 | tf_op jit(solution)/shard_map/all_to_all | solution.py:172
  271.8 2.3 copy-start.13
  271.8 3.2 copy-start.32
  275.0 27.7 %copy-start.5 = (f32[1024,1024]{0,1:T(8,128)}, f32[1024,1024]{0,1:T(8,128)S(1)}, u32[]{:S(2)}) copy-start(f32[1024,1024]{0,1:T(8,128)S(1)} %get-tuple-element.317) | copy-start | bytes 12582916
  280.8 28.3 %copy-start.3 = (f32[1024,2048]{0,1:T(8,128)}, f32[1024,2048]{0,1:T(8,128)S(1)}, u32[]{:S(2)}) copy-start(f32[1024,2048]{0,1:T(8,128)S(1)} %get-tuple-element.315) | copy-start | bytes 25165828
  292.1 25.8 %copy-start.4 = (f32[1024,2048]{0,1:T(8,128)}, f32[1024,2048]{0,1:T(8,128)S(1)}, u32[]{:S(2)}) copy-start(f32[1024,2048]{0,1:T(8,128)S(1)} %get-tuple-element.307) | copy-start | bytes 25165828
  295.2 28.8 %copy-start.2 = (f32[1024,2048]{0,1:T(8,128)}, f32[1024,2048]{0,1:T(8,128)S(1)}, u32[]{:S(2)}) copy-start(f32[1024,2048]{0,1:T(8,128)S(1)} %get-tuple-element.305) | copy-start | bytes 25165828
  299.9 2.2 copy-start.11
  303.5 17.2 %copy-start.24 = (f32[1024,128]{1,0:T(8,128)}, f32[1024,128]{1,0:T(8,128)S(1)}, u32[]{:S(2)}) copy-start(f32[1024,128]{1,0:T(8,128)S(1)} %fusion.65) | copy-start | bytes 1572868
  304.3 17.0 %copy-start.28 = (f32[1024,128]{1,0:T(8,128)}, f32[1024,128]{1,0:T(8,128)S(1)}, u32[]{:S(2)}) copy-start(f32[1024,128]{1,0:T(8,128)S(1)} %fusion.69) | copy-start | bytes 1572868
  310.4 10.3 %copy-start.16 = (f32[1024,128]{1,0:T(8,128)}, f32[1024,128]{1,0:T(8,128)S(1)}, u32[]{:S(2)}) copy-start(f32[1024,128]{1,0:T(8,128)S(1)} %fusion.34) | copy-start | bytes 1572868
  310.4 5.0 %copy-start.7 = (f32[1024,1024]{0,1:T(8,128)S(1)}, f32[1024,1024]{0,1:T(8,128)}, u32[]{:S(2)}) copy-start(f32[1024,1024]{0,1:T(8,128)} %get-tuple-element.309) | copy-start | bytes 12582916
  315.3 6.0 %copy-start.20 = (f32[1024,128]{1,0:T(8,128)}, f32[1024,128]{1,0:T(8,128)S(1)}, u32[]{:S(2)}) copy-start(f32[1024,128]{1,0:T(8,128)S(1)} %fusion.37) | copy-start | bytes 1572868
  316.8 5.1 %copy-start.26 = (f32[1024,128]{1,0:T(8,128)}, f32[1024,128]{1,0:T(8,128)S(1)}, u32[]{:S(2)}) copy-start(f32[1024,128]{1,0:T(8,128)S(1)} %fusion.61) | copy-start | bytes 1572868
  319.5 2.4 copy-start.18
  319.5 3.0 copy-start.9
  366.0 2.9 copy-start.12
  366.0 4.2 copy-start.10
  368.9 2.0 copy-start.21
  368.9 2.0 copy-start.23
  368.9 2.0 copy-start.29
  368.9 2.0 copy-start.31
  369.6 2.6 copy-start.8
  370.9 2.5 copy-start.6
  372.2 1.9 copy-start.17
  372.2 1.9 copy-start.19
  372.2 1.9 copy-start.25
  372.2 1.9 copy-start.27
  374.8 1.6 copy-start.14
  385.8 4.4 slice-start.10
  386.6 3.7 slice-start.11
  387.9 3.9 slice-start.4
  389.5 5.3 %slice-start.6 = ((s8[8388608]{0:T(1024)(128)(4,1)}), s8[4194304]{0:T(1024)(128)(4,1)S(1)}, s32[]{:S(2)}) async-start(s8[8388608]{0:T(1024)(128)(4,1)} %bitcast.149), calls=%async_computation.13 | async-start | bytes 8388608
  390.3 3.0 slice-start.5
  390.3 4.5 slice-start.7
  393.3 3.0 slice-start
  394.8 2.4 slice-start.1
  399.7 35.3 %all-to-all-start.6 = ((f32[16,128,128]{2,1,0:T(8,128)}), f32[16,128,128]{2,1,0:T(8,128)}, u32[]{:S(2)}, u32[]{:S(2)}) async-start(f32[16,128,128]{2,1,0:T(8,128)} %bitcast.191), calls=%async_computation.6 | async-start | bytes 2097152 | tf_op jit(solution)/shard_map/all_to_all | solution.py:217
  404.2 5.1 %copy-start.39 = (bf16[128,16,128]{2,0,1:T(8,128)(2,1)S(1)}, bf16[128,16,128]{2,0,1:T(8,128)(2,1)}, u32[]{:S(2)}) copy-start(bf16[128,16,128]{2,0,1:T(8,128)(2,1)} %copy-done.38) | copy-start | bytes 1572868
  409.4 1.6 copy-start.15
  409.4 1.7 copy-start.33
  411.0 6.5 %slice-start.8 = ((s8[8388608]{0:T(1024)(128)(4,1)}), s8[4194304]{0:T(1024)(128)(4,1)S(1)}, s32[]{:S(2)}) async-start(s8[8388608]{0:T(1024)(128)(4,1)} %bitcast.151), calls=%async_computation.15 | async-start | bytes 8388608
  412.3 5.2 %slice-start.9 = ((s8[8388608]{0:T(1024)(128)(4,1)}), s8[4194304]{0:T(1024)(128)(4,1)S(1)}, s32[]{:S(2)}) async-start(s8[8388608]{0:T(1024)(128)(4,1)} %bitcast.151), calls=%async_computation.16 | async-start | bytes 8388608
  420.6 2.0 copy-start.35
  422.7 3.7 slice-start.2
  424.0 1.6 copy-start.42
  424.0 2.7 slice-start.3
  426.7 3.7 copy-start.34
  430.4 11.6 %copy-start.43 = (bf16[1024,128]{1,0:T(8,128)(2,1)S(1)}, bf16[1024,128]{1,0:T(8,128)(2,1)}, u32[]{:S(2)}) copy-start(bf16[1024,128]{1,0:T(8,128)(2,1)} %fusion.25) | copy-start | bytes 786436
  430.4 11.7 %copy-start.40 = (bf16[128,16,128]{2,0,1:T(8,128)(2,1)S(1)}, bf16[128,16,128]{2,0,1:T(8,128)(2,1)}, u32[]{:S(2)}) copy-start(bf16[128,16,128]{2,0,1:T(8,128)(2,1)} %copy-done.38) | copy-start | bytes 1572868
  435.0 25.1 %all-to-all-start.5 = ((f32[16,128,128]{2,1,0:T(8,128)}), f32[16,128,128]{2,1,0:T(8,128)S(1)}, u32[]{:S(2)}, u32[]{:S(2)}) async-start(f32[16,128,128]{2,1,0:T(8,128)} %bitcast.44), calls=%async_computation.5 | async-start | bytes 2097152 | tf_op jit(solution)/shard_map/all_to_all | solution.py:216
  442.1 3.7 copy-start.37
  460.1 33.0 %all-to-all-start.4 = ((bf16[16,128,512]{2,1,0:T(8,128)(2,1)}), bf16[16,128,512]{2,1,0:T(8,128)(2,1)S(1)}, u32[]{:S(2)}, u32[]{:S(2)}) async-start(bf16[16,128,512]{2,1,0:T(8,128)(2,1)} %pad_maximum_fusion), calls=%async_computation.4 | async-start | bytes 4194304 | tf_op jit(solution)/shard_map/all_to_all | solution.py:214
  463.8 30.8 %copy-start.1 = (bf16[128,1024]{1,0:T(8,128)(2,1)S(1)}, bf16[128,1024]{1,0:T(8,128)(2,1)}, u32[]{:S(2)}) copy-start(bf16[128,1024]{1,0:T(8,128)(2,1)} %param.14) | copy-start | bytes 786436
  (5 other events, 5.9 us)
where the time goes:
time: 502 us; the launch traced here: 495 us
  blocking collectives  109 us (22%)
  matrix products  97.7 us (19%)
  local copies, waits for them, and re-layouts  92.4 us (18%)
  loops' own time  68.9 us (14%)
  waiting for transfers between devices  52.8 us (11%)
  starting transfers between devices  43 us (9%)
  other arithmetic  27.4 us (5%)
    another operation x2, loops' own time, suffix_from(): lax.scan(fold_element, initial, (jnp.arange(length), factors, offsets), r...  68.9 us
    dynamic_slice x96, local copies, waits for them, and re-layouts, suffix_from(): lax.scan(fold_element, initial, (jnp.arange(length), factors, offsets), r...  57.7 us
    unnamed x1, blocking collectives  51.3 us
    psum x1, blocking collectives, body(): value_error = lax.psum(estimate - placed, 'dp')  39.3 us
    dot_general x8, matrix products, head_probs(): jnp.dot(query_rows, key_rows.T, preferred_element_type=jnp.float32)  25.9 us
    all_to_all x1, waiting for transfers between devices, body(): lax.all_to_all(grad_query_heads, 'dp', split_axis=0, concat_axis=1, tiled...  20.8 us
    dot_general x8, matrix products, head_backward(): jnp.dot(grad_rows, value_head[:row_end].T, preferred_element_type=jnp.flo...  19.9 us
    unnamed x130, local copies, waits for them, and re-layouts  19.1 us
  transfers between devices with their start and end apart: 8, of which 4 were waited for; matrix products, arithmetic and copies ran while one was open for 35% of the time, Pallas kernels for 0%

commit v1 on v0

v1 whole, which is shorter than its diff:
```python
import math

import jax
import jax.numpy as jnp
from jax import lax
from jax.experimental import pallas as pl
from jax.experimental.pallas import tpu as pltpu
from jax.sharding import PartitionSpec as P

MESH = pl.DeviceIdType.MESH
F32, BF16 = jnp.float32, jnp.bfloat16
D = 128
PEERS = 8
GROUP = 8
ROWS = PEERS * D
KEYS = 2 * ROWS
T = 256
NB = ROWS // T
SPLIT = 4
HEADS = GROUP // SPLIT
WIDE = HEADS * D
BIG = 1e30
SCALE = 1.0 / math.sqrt(D)
EXP2 = SCALE * math.log2(math.e)


def mm(a, b, dims=((1,), (0,))):
    return lax.dot_general(a, b, (dims, ((), ())), preferred_element_type=F32)


def ds(start, size):
    if isinstance(start, int):
        return pl.ds(start, size)
    return pl.ds(pl.multiple_of(start, size), size)


def kernel(
    q_in, k_in, v_in, g_in, readout_in, rewards_in, saved_in, ends_in, segs_in,
    dq_out, dk_out, dv_out, adv_out,
    q, g, dq, kaug, v, kt, vt, qm, probs, ohi, olo, dsc, sc, dka, dva, dkb, dvb, rk, rv,
    pk, tot, est, es, inv, rcol, vet, rd,
    q_s, q_r, g_s, g_r, d_s, d_r, kv_s, kv_r, x_s, x_r, pk_s, pk_r, tot_s, tot_r, es_s, es_r, o_s, o_r, loc,
):
    me = lax.axis_index("dp")
    sq = lax.axis_index("seq")
    seqs = lax.axis_size("seq")
    x = lax.div(me, PEERS)
    hd = lax.rem(me, PEERS)
    late = x == 1

    def dev(half, place):
        return (half * PEERS + place, sq)

    def nxt(k):
        return lax.rem(hd + k, PEERS)

    def send(src, dst, ssem, rsem, device):
        return pltpu.make_async_remote_copy(
            src_ref=src, dst_ref=dst, send_sem=ssem, recv_sem=rsem, device_id=device, device_id_type=MESH
        )

    barrier = pltpu.get_barrier_semaphore()
    for k in range(1, 16):
        pl.semaphore_signal(barrier, inc=1, device_id=(lax.rem(me + k, 16), sq), device_id_type=MESH)
    for k in (1, seqs - 1):
        pl.semaphore_signal(barrier, inc=1, device_id=(me, lax.rem(sq + k, seqs)), device_id_type=MESH)
    pl.semaphore_wait(barrier, 17)

    def kv_copy(k, t):
        src, dst = ((k_in, kaug), (v_in, v))[t]
        p = nxt(k)
        return send(
            src.at[:, ds(p * D, D)], dst.at[ds(ROWS + hd * D, D), pl.ds(0, D)], kv_s.at[t, k], kv_r.at[t, k], dev(x, p)
        )

    def kv_local(t):
        src, dst = ((k_in, kaug), (v_in, v))[t]
        return pltpu.make_async_copy(src.at[:, ds(hd * D, D)], dst.at[ds(ROWS + hd * D, D), pl.ds(0, D)], kv_r.at[t, 0])

    def in_copy(src, dst, ssem, rsem, part, k):
        p = nxt(k)
        return send(
            src.at[:, ds((p * SPLIT + part) * WIDE, WIDE)],
            dst.at[ds(hd * D, D), ds(part * WIDE, WIDE)],
            ssem.at[part, k], rsem.at[part, k], dev(x, p),
        )

    def in_local(src, dst, rsem, part):
        return pltpu.make_async_copy(
            src.at[:, ds((hd * SPLIT + part) * WIDE, WIDE)], dst.at[ds(hd * D, D), ds(part * WIDE, WIDE)], rsem.at[part, 0]
        )

    def start_in(src, dst, ssem, rsem, part):
        in_local(src, dst, rsem, part).start()
        for k in range(1, PEERS):
            in_copy(src, dst, ssem, rsem, part, k).start()

    def wait_in(src, dst, ssem, rsem, part):
        in_local(src, dst, rsem, part).wait()
        for k in range(1, PEERS):
            in_copy(src, dst, ssem, rsem, part, k).wait_recv()

    for t in range(2):
        kv_local(t).start()
        for k in range(1, PEERS):
            kv_copy(k, t).start()

    sub = lax.broadcasted_iota(jnp.int32, (D, D), 0)
    lane = lax.broadcasted_iota(jnp.int32, (D, D), 1)
    lane_f = lane.astype(F32)

    def wide(row):
        return jnp.broadcast_to(row, (D, D))

    def column(row):
        return wide(row).T

    last = jnp.logical_and(me == 15, jnp.logical_or(sq == seqs // 2 - 1, sq == seqs - 1))
    ends = ends_in[...].astype(F32)
    row_lane = lax.broadcasted_iota(jnp.int32, (1, D), 1)
    ends = jnp.where(jnp.logical_and(row_lane == D - 1, last), 1.0, ends)
    ends_col = column(ends)
    before = jnp.sum(jnp.where(sub < lane, ends_col, 0.0), axis=0, keepdims=True)
    total_ends = jnp.sum(ends, axis=1, keepdims=True)
    reach = jnp.logical_and(sub >= lane, column(before) == wide(before))
    local_gain = jnp.sum(jnp.where(reach, column(rewards_in[...]), 0.0), axis=0, keepdims=True)
    passing = (total_ends - before == 0).astype(F32)
    through = (total_ends == 0).astype(F32)
    pk[me, 0:1, :] = segs_in[...].astype(F32)
    pk[me, 1:2, :] = jnp.broadcast_to(through, (1, D))
    pk[me, 2:3, :] = jnp.broadcast_to(local_gain[:, 0:1], (1, D))

    def pk_copy(k):
        return send(pk.at[me], pk.at[me], pk_s.at[k], pk_r.at[k], (lax.rem(me + k, 16), sq))

    for k in range(1, 16):
        pk_copy(k).start()

    start_in(q_in, q, q_s, q_r, 0)
    start_in(q_in, q, q_s, q_r, 1)

    for h in range(GROUP):
        rcol[h] = column(readout_in[h : h + 1, :])
    est[...] = jnp.zeros_like(est)
    dka[...] = jnp.zeros_like(dka)
    dva[...] = jnp.zeros_like(dva)

    for k in range(1, 16):
        pk_copy(k).wait()

    def fold(value, lowest):
        for d in range(15, -1, -1):
            joined = pk[d, 2:3, :] + pk[d, 1:2, :] * value
            value = joined if lowest is None else jnp.where(d >= lowest, joined, value)
        return value

    tot[0] = jnp.broadcast_to(fold(jnp.zeros((1, D), F32), None), (8, D))
    tot_copy = send(tot.at[0], tot.at[1], tot_s, tot_r, (me, lax.rem(sq + seqs - 1, seqs)))
    tot_copy.start()

    for t in range(2):
        kv_local(t).wait()
        for k in range(1, PEERS):
            kv_copy(k, t).wait_recv()

    def x_copy(t):
        dst = (kaug, v)[t]
        return send(
            dst.at[pl.ds(ROWS, ROWS), pl.ds(0, D)], dst.at[pl.ds(0, ROWS), pl.ds(0, D)], x_s.at[t], x_r.at[t], dev(1 - x, hd)
        )

    @pl.when(x == 0)
    def _():
        for t in range(2):
            x_copy(t).start()
        kaug[0:ROWS, 0:D] = jnp.zeros((ROWS, D), BF16)
        v[0:ROWS, :] = jnp.zeros((ROWS, D), BF16)

    start_in(q_in, q, q_s, q_r, 2)
    start_in(q_in, q, q_s, q_r, 3)

    first = pk[0, 0:1, 0:1]

    def seg_block(b, carry):
        own = b >= PEERS
        place = jnp.where(own, x * PEERS + b - PEERS, (1 - x) * PEERS + b)
        code = column(pk[place, 0:1, :] - first)
        hidden = jnp.logical_and(jnp.logical_not(own), x == 0)
        code = jnp.where(hidden, 100.0, code)
        kaug[ds(b * D, D), D : 2 * D] = jnp.where(code == lane_f, 1.0, 0.0).astype(BF16)
        return carry

    lax.fori_loop(0, 2 * PEERS, seg_block, 0)

    def row_block(b, carry):
        code = column(pk[x * PEERS + b, 0:1, :] - first)
        qm[ds(b * D, D), :] = jnp.where(code == lane_f, 0.0, -BIG).astype(BF16)
        return carry

    lax.fori_loop(0, PEERS, row_block, 0)

    @pl.when(late)
    def _():
        for t in range(2):
            x_copy(t).wait_recv()

    for b in range(2 * PEERS):
        kt[:, b * D : (b + 1) * D] = kaug[b * D : (b + 1) * D, 0:D].T
        vt[:, b * D : (b + 1) * D] = v[b * D : (b + 1) * D, :].T

    tile_sub = lax.broadcasted_iota(jnp.int32, (T, T), 0)
    tile_lane = lax.broadcasted_iota(jnp.int32, (T, T), 1)

    def forward(h):
        cols = ds(h * D, D)
        for i in range(NB):
            r = slice(i * T, (i + 1) * T)
            count = NB + i + 1
            qa = jnp.concatenate([q[r, cols], qm[r, :]], axis=1)
            top = None
            for j in range(count):
                s = mm(kaug[j * T : (j + 1) * T, :], qa, ((1,), (1,)))
                if j == count - 1:
                    s = jnp.where(tile_sub <= tile_lane, s, -BIG)
                sc[i % 2, j * T : (j + 1) * T, :] = s
                part = jnp.max(s.reshape(T // 8, 8, T), axis=0)
                top = part if top is None else jnp.maximum(top, part)
            top = jnp.max(top, axis=0, keepdims=True) * EXP2
            total = None
            for j in range(count):
                p = jnp.exp2(sc[i % 2, j * T : (j + 1) * T, :] * EXP2 - top)
                part = jnp.sum(p.reshape(T // 8, 8, T), axis=0)
                total = part if total is None else total + part
                probs[h, j * T : (j + 1) * T, r] = p.astype(BF16)
            scale = 1.0 / jnp.sum(total, axis=0, keepdims=True)
            n = count * T
            out = mm(vt[:, 0:n], probs[h, 0:n, r]) * scale
            high = out.astype(BF16)
            ohi[h, :, r] = high
            olo[h, :, r] = (out - high.astype(F32)).astype(BF16)
            for c in range(T // D):
                b = i * (T // D) + c
                half = slice(c * D, (c + 1) * D)
                est[b : b + 1, :] += jnp.sum(out[:, half] * rcol[h], axis=0, keepdims=True)
                inv[h, b : b + 1, :] = scale[:, half]

    def forward_part(part, carry):
        wait_in(q_in, q, q_s, q_r, part)

        @pl.when(part >= 1)
        def _():
            start_in(g_in, g, g_s, g_r, part - 1)

        lax.fori_loop(0, HEADS, lambda n, c: (forward(part * HEADS + n), c)[1], 0)
        return carry

    lax.fori_loop(0, SPLIT, forward_part, 0)

    tot_copy.wait()
    beyond = tot[1, 0:1, :]
    gains = local_gain + passing * fold(beyond, me + 1)
    adv_out[...] = gains - saved_in[...]
    place_sub = lax.broadcasted_iota(jnp.int32, (PEERS, D), 0)
    es[hd] = est[...] - jnp.where(place_sub == hd, jnp.broadcast_to(gains, (PEERS, D)), 0.0)

    def es_copy(k):
        return send(es.at[hd], es.at[hd], es_s.at[k], es_r.at[k], dev(x, nxt(k)))

    for k in range(1, PEERS):
        es_copy(k).start()
    start_in(g_in, g, g_s, g_r, SPLIT - 1)
    for k in range(1, PEERS):
        es_copy(k).wait()
    error = es[0]
    for d in range(1, PEERS):
        error = error + es[d]
    vet[...] = jnp.concatenate([error] * (D // PEERS), axis=0).T

    def backward(h):
        cols = ds(h * D, D)
        scales = jnp.concatenate([inv[h]] * (D // PEERS), axis=0).T
        readout = readout_in[pl.ds(h, 1), :]
        for b in range(PEERS):
            r = slice(b * D, (b + 1) * D)
            grad = g[r, cols].astype(F32) + vet[:, b : b + 1] * readout
            grad = (grad * scales[:, b : b + 1]).astype(BF16)
            g[r, cols] = grad
            cross = mm(grad, ohi[h, :, r]) + mm(grad, olo[h, :, r])
            rd[:, r] = jnp.broadcast_to(jnp.sum(jnp.where(sub == lane, cross, 0.0), axis=0, keepdims=True), (8, D))
        for i in range(NB):
            r = slice(i * T, (i + 1) * T)
            count = NB + i + 1
            grad = g[r, cols]
            dot = rd[0:1, r]
            for j in range(count):
                a = slice(j * T, (j + 1) * T)
                dp = mm(v[a, :], grad, ((1,), (1,)))
                dsc[a, r] = (probs[h, a, r].astype(F32) * (dp - dot)).astype(BF16)
            n = count * T
            out = mm(kt[:, 0:n], dsc[0:n, r]) * SCALE
            dq[r, cols] = out.T.astype(BF16)
        for j in range(2 * NB):
            a = slice(j * T, (j + 1) * T)
            low = max(0, j - NB) * T
            dva[a, :] += mm(probs[h, a, low:ROWS], g[low:ROWS, cols])
            dka[a, :] += mm(dsc[a, low:ROWS], q[low:ROWS, cols])

    def dq_copy(part, k):
        p = nxt(k)
        return send(
            dq.at[ds(p * D, D), ds(part * WIDE, WIDE)],
            dq_out.at[:, ds((hd * SPLIT + part) * WIDE, WIDE)],
            d_s.at[part, k], d_r.at[part, k], dev(x, p),
        )

    def dq_local(part):
        return pltpu.make_async_copy(
            dq.at[ds(hd * D, D), ds(part * WIDE, WIDE)], dq_out.at[:, ds((hd * SPLIT + part) * WIDE, WIDE)], d_r.at[part, 0]
        )

    def backward_part(part, carry):
        wait_in(g_in, g, g_s, g_r, part)
        lax.fori_loop(0, HEADS, lambda n, c: (backward(part * HEADS + n), c)[1], 0)
        dq_local(part).start()
        for k in range(1, PEERS):
            dq_copy(part, k).start()
        return carry

    lax.fori_loop(0, SPLIT, backward_part, 0)

    dkb[...] = (dka[...] * SCALE).astype(BF16)
    dvb[...] = dva[...].astype(BF16)

    def out_copy(t, k, same):
        src, dst = ((dkb, rk), (dvb, rv))[t]
        p = nxt(k)
        base = ROWS if same else 0
        slot = 1 if same else 0
        index = k + (0 if same else PEERS)
        return send(
            src.at[ds(base + p * D, D), :], dst.at[slot, :, ds(hd * D, D)], o_s.at[t, index], o_r.at[t, index],
            dev(x if same else 1 - x, p),
        )

    @pl.when(late)
    def _():
        for k in range(PEERS):
            for t in range(2):
                out_copy(t, k, False).start()

    def out_local(t):
        src, dst = ((dkb, rk), (dvb, rv))[t]
        return pltpu.make_async_copy(src.at[ds(ROWS + hd * D, D), :], dst.at[1, :, ds(hd * D, D)], loc.at[t])

    for t in range(2):
        out_local(t).start()
        for k in range(1, PEERS):
            out_copy(t, k, True).start()
    for t in range(2):
        out_local(t).wait()
        for k in range(1, PEERS):
            out_copy(t, k, True).wait()

    @pl.when(late)
    def _():
        for t in range(2):
            for k in range(PEERS):
                out_copy(t, k, False).wait_send()
        dk_out[...] = rk[1]
        dv_out[...] = rv[1]

    @pl.when(x == 0)
    def _():
        for t in range(2):
            for k in range(PEERS):
                out_copy(t, k, False).wait_recv()
            x_copy(t).wait_send()
        dk_out[...] = (rk[0].astype(F32) + rk[1].astype(F32)).astype(BF16)
        dv_out[...] = (rv[0].astype(F32) + rv[1].astype(F32)).astype(BF16)

    for t in range(2):
        for k in range(1, PEERS):
            kv_copy(k, t).wait_send()
    for part in range(SPLIT):
        dq_local(part).wait()
        for k in range(1, PEERS):
            in_copy(q_in, q, q_s, q_r, part, k).wait_send()
            in_copy(g_in, g, g_s, g_r, part, k).wait_send()
            dq_copy(part, k).wait()


def body(queries, keys, values, cotangent, readout, rewards, saved, ends, segs):
    place = lax.rem(lax.axis_index("dp"), PEERS)
    heads = lax.dynamic_slice_in_dim(readout.reshape(PEERS * GROUP, D), place * GROUP, GROUP, 0).astype(F32)
    vmem = pl.BlockSpec(memory_space=pltpu.VMEM)
    hbm = pl.BlockSpec(memory_space=pl.ANY)
    dma = pltpu.SemaphoreType.DMA
    grads = pl.pallas_call(
        kernel,
        out_shape=(
            jax.ShapeDtypeStruct(queries.shape, BF16),
            jax.ShapeDtypeStruct(keys.shape, BF16),
            jax.ShapeDtypeStruct(values.shape, BF16),
            jax.ShapeDtypeStruct((1, D), F32),
        ),
        in_specs=[hbm, hbm, hbm, hbm, vmem, vmem, vmem, vmem, vmem],
        out_specs=(hbm, vmem, vmem, vmem),
        scratch_shapes=[
            pltpu.VMEM((ROWS, ROWS), BF16),
            pltpu.VMEM((ROWS, ROWS), BF16),
            pltpu.VMEM((ROWS, ROWS), BF16),
            pltpu.VMEM((KEYS, 2 * D), BF16),
            pltpu.VMEM((KEYS, D), BF16),
            pltpu.VMEM((D, KEYS), BF16),
            pltpu.VMEM((D, KEYS), BF16),
            pltpu.VMEM((ROWS, D), BF16),
            pltpu.VMEM((GROUP, KEYS, ROWS), BF16),
            pltpu.VMEM((GROUP, D, ROWS), BF16),
            pltpu.VMEM((GROUP, D, ROWS), BF16),
            pltpu.VMEM((KEYS, ROWS), BF16),
            pltpu.VMEM((2, KEYS, T), F32),
            pltpu.VMEM((KEYS, D), F32),
            pltpu.VMEM((KEYS, D), F32),
            pltpu.VMEM((KEYS, D), BF16),
            pltpu.VMEM((KEYS, D), BF16),
            pltpu.VMEM((2, D, ROWS), BF16),
            pltpu.VMEM((2, D, ROWS), BF16),
            pltpu.VMEM((16, 8, D), F32),
            pltpu.VMEM((2, 8, D), F32),
            pltpu.VMEM((PEERS, D), F32),
            pltpu.VMEM((PEERS, PEERS, D), F32),
            pltpu.VMEM((GROUP, PEERS, D), F32),
            pltpu.VMEM((GROUP, D, D), F32),
            pltpu.VMEM((D, D), F32),
            pltpu.VMEM((8, ROWS), F32),
            dma((SPLIT, PEERS)), dma((SPLIT, PEERS)),
            dma((SPLIT, PEERS)), dma((SPLIT, PEERS)),
            dma((SPLIT, PEERS)), dma((SPLIT, PEERS)),
            dma((2, PEERS)), dma((2, PEERS)),
            dma((2,)), dma((2,)),
            dma((16,)), dma((16,)),
            dma, dma,
            dma((PEERS,)), dma((PEERS,)),
            dma((2, 2 * PEERS)), dma((2, 2 * PEERS)),
            dma((2,)),
        ],
        compiler_params=pltpu.CompilerParams(
            collective_id=0, has_side_effects=True, vmem_limit_bytes=62 << 20
        ),
    )(
        queries, keys, values, cotangent, heads,
        rewards.reshape(1, D), saved.reshape(1, D), ends.reshape(1, D), segs.reshape(1, D),
    )
    return (grads[0], grads[1], grads[2], grads[3].reshape(D))


def solution(mesh):
    rows, flat = P(("seq", "dp"), None), P(("seq", "dp"))
    return jax.shard_map(
        body,
        mesh=mesh,
        in_specs=(rows, rows, rows, rows, P(), flat, flat, flat, flat),
        out_specs=(rows, rows, rows, flat),
        check_vma=False,
    )
```

time: 502 us -> 126 us (0.25)
  the two profiles are of different devices: /device:TPU:24 before, /device:TPU:1 now
where the time goes in v1:
time: 126 us
  Pallas kernels  119 us (94%)
  local copies, waits for them, and re-layouts  5.08 us (4%)
  other arithmetic  1.28 us (1%)
    pallas_call x1, Pallas kernels, body(): pl.pallas_call(kernel, out_shape=(jax.ShapeDtypeStruct(queries.shape, BF1...  119 us
    unnamed x10, local copies, waits for them, and re-layouts  5.08 us

profile of v1, /device:TPU:1, one launch (start us, length us, event | category | flops | bytes accessed | tf_op | source)
XLA Modules:
  0.0 126.1 jit_solution(13133190979117966786)
XLA Ops:
  0.6 1.3 %dynamic-slice_convert_fusion.readout_in = f32[8,128]{1,0:T(8,128)} fusion(bf16[64,128]{1,0:T(8,128)(2,1)} %bitcast.10, s32[]{:T(128)S(6)} %select_n.3), kind=kLoop, calls=%fused_computation | loop fusion | flops 1024 | bytes 6148 | tf_op jit(solution)/shard_map/convert_element_type | solution.py:394
  1.9 119.0 %shard_map.120 = (bf16[128,8192]{1,0:T(8,128)(2,1)}, bf16[128,1024]{1,0:T(8,128)(2,1)}, bf16[128,1024]{1,0:T(8,128)(2,1)}, f32[1,128]{1,0:T(1,128)}) custom-call(bf16[128,8192]{1,0:T(8,128)(2,1)} %q_in.1, bf16[128,1024]{1,0:T(8,128)(2,1)} %k_in.1, bf16[128,1024]{1,0:T(8,128)(2,1)} %v_in.1, bf16[128,8192]{1,0:T(8,128)(2,1)} %g_in.1, ...), custom_call_target="tpu_custom_call" | custom-call | tf_op jit(solution)/shard_map/pallas_call | solution.py:398
  121.0 0.0 copy-start.1
  121.0 0.0 copy-start
  121.0 0.0 copy-start.2
  121.0 3.1 %copy.17 = bf16[128,8192]{1,0:T(8,128)(2,1)} copy(bf16[128,8192]{1,0:T(8,128)(2,1)} %get-tuple-element.16) | data formatting | bytes 4194304
  124.2 0.0 copy-done.1
  124.2 0.7 copy.18
  124.9 0.0 copy-done
  124.9 0.7 copy.19
  125.6 0.0 copy-done.2
  125.6 0.5 copy.20
Async XLA Ops:
  121.0 3.2 %copy-start.1 = (bf16[128,1024]{1,0:T(8,128)(2,1)S(1)}, bf16[128,1024]{1,0:T(8,128)(2,1)}, u32[]{:S(2)}) copy-start(bf16[128,1024]{1,0:T(8,128)(2,1)} %get-tuple-element.17) | copy-start | bytes 786436
  121.0 3.9 %copy-start = (bf16[128,1024]{1,0:T(8,128)(2,1)S(1)}, bf16[128,1024]{1,0:T(8,128)(2,1)}, u32[]{:S(2)}) copy-start(bf16[128,1024]{1,0:T(8,128)(2,1)} %get-tuple-element.18) | copy-start | bytes 786436
  121.0 4.6 %copy-start.2 = (f32[1,128]{1,0:T(1,128)S(1)}, f32[1,128]{1,0:T(1,128)}, u32[]{:S(2)}) copy-start(f32[1,128]{1,0:T(1,128)} %get-tuple-element.11) | copy-start | bytes 1540

commit v2 on v1

--- a/solution.py
+++ b/solution.py
@@ -59,12 +59,14 @@
             src_ref=src, dst_ref=dst, send_sem=ssem, recv_sem=rsem, device_id=device, device_id_type=MESH
         )
 
+    def readout_row(h):
+        return readout_in[:, ds((hd * GROUP + h) * D, D)].astype(F32)
+
     barrier = pltpu.get_barrier_semaphore()
     for k in range(1, 16):
         pl.semaphore_signal(barrier, inc=1, device_id=(lax.rem(me + k, 16), sq), device_id_type=MESH)
     for k in (1, seqs - 1):
         pl.semaphore_signal(barrier, inc=1, device_id=(me, lax.rem(sq + k, seqs)), device_id_type=MESH)
-    pl.semaphore_wait(barrier, 17)
 
     def kv_copy(k, t):
         src, dst = ((k_in, kaug), (v_in, v))[t]
@@ -100,10 +102,12 @@
         for k in range(1, PEERS):
             in_copy(src, dst, ssem, rsem, part, k).wait_recv()
 
-    for t in range(2):
-        kv_local(t).start()
-        for k in range(1, PEERS):
-            kv_copy(k, t).start()
+    def x_copy(t, k):
+        src, dst = ((k_in, kaug), (v_in, v))[t]
+        p = nxt(k)
+        return send(
+            src.at[:, ds(p * D, D)], dst.at[ds(hd * D, D), pl.ds(0, D)], x_s.at[t, k], x_r.at[t, k], dev(1 - x, p)
+        )
 
     sub = lax.broadcasted_iota(jnp.int32, (D, D), 0)
     lane = lax.broadcasted_iota(jnp.int32, (D, D), 1)
@@ -133,14 +137,30 @@
     def pk_copy(k):
         return send(pk.at[me], pk.at[me], pk_s.at[k], pk_r.at[k], (lax.rem(me + k, 16), sq))
 
+    pl.semaphore_wait(barrier, 17)
     for k in range(1, 16):
         pk_copy(k).start()
-
-    start_in(q_in, q, q_s, q_r, 0)
-    start_in(q_in, q, q_s, q_r, 1)
+    for t in range(2):
+        kv_local(t).start()
+        for k in range(1, PEERS):
+            kv_copy(k, t).start()
+
+    @pl.when(x == 0)
+    def _():
+        for t in range(2):
+            for k in range(PEERS):
+                x_copy(t, k).start()
+
+    for part in range(SPLIT):
+        start_in(q_in, q, q_s, q_r, part)
+
+    @pl.when(x == 0)
+    def _():
+        kaug[0:ROWS, 0:D] = jnp.zeros((ROWS, D), BF16)
+        v[0:ROWS, :] = jnp.zeros((ROWS, D), BF16)
 
     for h in range(GROUP):
-        rcol[h] = column(readout_in[h : h + 1, :])
+        rcol[h] = column(readout_row(h))
     est[...] = jnp.zeros_like(est)
     dka[...] = jnp.zeros_like(dka)
     dva[...] = jnp.zeros_like(dva)
@@ -158,82 +178,63 @@
     tot_copy = send(tot.at[0], tot.at[1], tot_s, tot_r, (me, lax.rem(sq + seqs - 1, seqs)))
     tot_copy.start()
 
+    lines = [pk[(1 - x) * PEERS + b, 0:1, :] for b in range(PEERS)] + [pk[x * PEERS + b, 0:1, :] for b in range(PEERS)]
+    codes = (jnp.concatenate(lines * (D // 16), axis=0) - pk[0, 0:1, 0:1]).T
+    for b in range(2 * PEERS):
+        code = jnp.broadcast_to(codes[:, b : b + 1], (D, D))
+        if b < PEERS:
+            code = jnp.where(x == 0, 100.0, code)
+        else:
+            qm[(b - PEERS) * D : (b - PEERS + 1) * D, :] = jnp.where(code == lane_f, 0.0, -BIG).astype(BF16)
+        kaug[b * D : (b + 1) * D, D : 2 * D] = jnp.where(code == lane_f, 1.0, 0.0).astype(BF16)
+
     for t in range(2):
         kv_local(t).wait()
         for k in range(1, PEERS):
             kv_copy(k, t).wait_recv()
-
-    def x_copy(t):
-        dst = (kaug, v)[t]
-        return send(
-            dst.at[pl.ds(ROWS, ROWS), pl.ds(0, D)], dst.at[pl.ds(0, ROWS), pl.ds(0, D)], x_s.at[t], x_r.at[t], dev(1 - x, hd)
-        )
-
-    @pl.when(x == 0)
-    def _():
-        for t in range(2):
-            x_copy(t).start()
-        kaug[0:ROWS, 0:D] = jnp.zeros((ROWS, D), BF16)
-        v[0:ROWS, :] = jnp.zeros((ROWS, D), BF16)
-
-    start_in(q_in, q, q_s, q_r, 2)
-    start_in(q_in, q, q_s, q_r, 3)
-
-    first = pk[0, 0:1, 0:1]
-
-    def seg_block(b, carry):
-        own = b >= PEERS
-        place = jnp.where(own, x * PEERS + b - PEERS, (1 - x) * PEERS + b)
-        code = column(pk[place, 0:1, :] - first)
-        hidden = jnp.logical_and(jnp.logical_not(own), x == 0)
-        code = jnp.where(hidden, 100.0, code)
-        kaug[ds(b * D, D), D : 2 * D] = jnp.where(code == lane_f, 1.0, 0.0).astype(BF16)
-        return carry
-
-    lax.fori_loop(0, 2 * PEERS, seg_block, 0)
-
-    def row_block(b, carry):
-        code = column(pk[x * PEERS + b, 0:1, :] - first)
-        qm[ds(b * D, D), :] = jnp.where(code == lane_f, 0.0, -BIG).astype(BF16)
-        return carry
-
-    lax.fori_loop(0, PEERS, row_block, 0)
 
     @pl.when(late)
     def _():
         for t in range(2):
-            x_copy(t).wait_recv()
+            for k in range(PEERS):
+                x_copy(t, k).wait_recv()
 
     for b in range(2 * PEERS):
-        kt[:, b * D : (b + 1) * D] = kaug[b * D : (b + 1) * D, 0:D].T
         vt[:, b * D : (b + 1) * D] = v[b * D : (b + 1) * D, :].T
 
     tile_sub = lax.broadcasted_iota(jnp.int32, (T, T), 0)
     tile_lane = lax.broadcasted_iota(jnp.int32, (T, T), 1)
 
-    def forward(h):
-        cols = ds(h * D, D)
-        for i in range(NB):
+    def forward(heads):
+        steps = [(h, i) for h in heads for i in range(NB)]
+        state = {}
+
+        def score(t, j):
+            h, i = steps[t]
+            cols, r = ds(h * D, D), slice(i * T, (i + 1) * T)
+            if j == 0:
+                state["q", t] = jnp.concatenate([q[r, cols], qm[r, :]], axis=1)
+            s = mm(kaug[j * T : (j + 1) * T, :], state["q", t], ((1,), (1,)))
+            if j == NB + i:
+                s = jnp.where(tile_sub <= tile_lane, s, -BIG)
+            sc[t % 2, j * T : (j + 1) * T, :] = s
+            part = jnp.max(s.reshape(T // 8, 8, T), axis=0)
+            state["top", t] = part if j == 0 else jnp.maximum(state["top", t], part)
+            if j == NB + i:
+                state["top", t] = jnp.max(state["top", t], axis=0, keepdims=True) * EXP2
+
+        def weigh(t, j):
+            h, i = steps[t]
             r = slice(i * T, (i + 1) * T)
-            count = NB + i + 1
-            qa = jnp.concatenate([q[r, cols], qm[r, :]], axis=1)
-            top = None
-            for j in range(count):
-                s = mm(kaug[j * T : (j + 1) * T, :], qa, ((1,), (1,)))
-                if j == count - 1:
-                    s = jnp.where(tile_sub <= tile_lane, s, -BIG)
-                sc[i % 2, j * T : (j + 1) * T, :] = s
-                part = jnp.max(s.reshape(T // 8, 8, T), axis=0)
-                top = part if top is None else jnp.maximum(top, part)
-            top = jnp.max(top, axis=0, keepdims=True) * EXP2
-            total = None
-            for j in range(count):
-                p = jnp.exp2(sc[i % 2, j * T : (j + 1) * T, :] * EXP2 - top)
-                part = jnp.sum(p.reshape(T // 8, 8, T), axis=0)
-                total = part if total is None else total + part
-                probs[h, j * T : (j + 1) * T, r] = p.astype(BF16)
-            scale = 1.0 / jnp.sum(total, axis=0, keepdims=True)
-            n = count * T
+            p = jnp.exp2(sc[t % 2, j * T : (j + 1) * T, :] * EXP2 - state["top", t])
+            part = jnp.sum(p.reshape(T // 8, 8, T), axis=0)
+            state["sum", t] = part if j == 0 else state["sum", t] + part
+            probs[h, j * T : (j + 1) * T, r] = p.astype(BF16)
+
+        def output(t):
+            h, i = steps[t]
+            r, n = slice(i * T, (i + 1) * T), (NB + i + 1) * T
+            scale = 1.0 / jnp.sum(state["sum", t], axis=0, keepdims=True)
             out = mm(vt[:, 0:n], probs[h, 0:n, r]) * scale
             high = out.astype(BF16)
             ohi[h, :, r] = high
@@ -244,14 +245,23 @@
                 est[b : b + 1, :] += jnp.sum(out[:, half] * rcol[h], axis=0, keepdims=True)
                 inv[h, b : b + 1, :] = scale[:, half]
 
+        for t in range(len(steps) + 2):
+            if t >= 2:
+                output(t - 2)
+            for j in range(2 * NB):
+                if t < len(steps) and j <= NB + steps[t][1]:
+                    score(t, j)
+                if 1 <= t <= len(steps) and j <= NB + steps[t - 1][1]:
+                    weigh(t - 1, j)
+
     def forward_part(part, carry):
         wait_in(q_in, q, q_s, q_r, part)
 
-        @pl.when(part >= 1)
+        @pl.when(part >= 2)
         def _():
-            start_in(g_in, g, g_s, g_r, part - 1)
-
-        lax.fori_loop(0, HEADS, lambda n, c: (forward(part * HEADS + n), c)[1], 0)
+            start_in(g_in, g, g_s, g_r, part - 2)
+
+        forward([part * HEADS + n for n in range(HEADS)])
         return carry
 
     lax.fori_loop(0, SPLIT, forward_part, 0)
@@ -268,7 +278,10 @@
 
     for k in range(1, PEERS):
         es_copy(k).start()
-    start_in(g_in, g, g_s, g_r, SPLIT - 1)
+    for part in range(SPLIT - 2, SPLIT):
+        start_in(g_in, g, g_s, g_r, part)
+    for b in range(2 * PEERS):
+        kt[:, b * D : (b + 1) * D] = kaug[b * D : (b + 1) * D, 0:D].T
     for k in range(1, PEERS):
         es_copy(k).wait()
     error = es[0]
@@ -276,77 +289,117 @@
         error = error + es[d]
     vet[...] = jnp.concatenate([error] * (D // PEERS), axis=0).T
 
-    def backward(h):
+    def prepare(n, h):
         cols = ds(h * D, D)
         scales = jnp.concatenate([inv[h]] * (D // PEERS), axis=0).T
-        readout = readout_in[pl.ds(h, 1), :]
-        for b in range(PEERS):
+        readout = readout_row(h)
+
+        def block(b):
             r = slice(b * D, (b + 1) * D)
             grad = g[r, cols].astype(F32) + vet[:, b : b + 1] * readout
             grad = (grad * scales[:, b : b + 1]).astype(BF16)
             g[r, cols] = grad
             cross = mm(grad, ohi[h, :, r]) + mm(grad, olo[h, :, r])
-            rd[:, r] = jnp.broadcast_to(jnp.sum(jnp.where(sub == lane, cross, 0.0), axis=0, keepdims=True), (8, D))
-        for i in range(NB):
-            r = slice(i * T, (i + 1) * T)
-            count = NB + i + 1
-            grad = g[r, cols]
-            dot = rd[0:1, r]
-            for j in range(count):
-                a = slice(j * T, (j + 1) * T)
-                dp = mm(v[a, :], grad, ((1,), (1,)))
-                dsc[a, r] = (probs[h, a, r].astype(F32) * (dp - dot)).astype(BF16)
-            n = count * T
-            out = mm(kt[:, 0:n], dsc[0:n, r]) * SCALE
-            dq[r, cols] = out.T.astype(BF16)
-        for j in range(2 * NB):
-            a = slice(j * T, (j + 1) * T)
-            low = max(0, j - NB) * T
+            rd[n, :, r] = jnp.broadcast_to(jnp.sum(jnp.where(sub == lane, cross, 0.0), axis=0, keepdims=True), (8, D))
+
+        return [(block, (b,)) for b in range(PEERS)]
+
+    def units(n, h, own):
+        cols = ds(h * D, D)
+        base = ROWS if own else 0
+
+        def grads(i, j):
+            r, a = slice(i * T, (i + 1) * T), slice(base + j * T, base + (j + 1) * T)
+            c = slice(n * ROWS + j * T, n * ROWS + (j + 1) * T)
+            dp = mm(v[a, :], g[r, cols], ((1,), (1,)))
+            dsc[c, r] = (probs[h, a, r].astype(F32) * (dp - rd[n, 0:1, r])).astype(BF16)
+            count = i + 1 if own else NB
+            if j == count - 1:
+                out = mm(kt[:, base : base + count * T], dsc[n * ROWS : n * ROWS + count * T, r])
+                keep = slice(i * D, (i + 1) * D)
+                if own:
+                    dq[r, cols] = ((sc[n, keep, :] + out) * SCALE).T.astype(BF16)
+                else:
+                    sc[n, keep, :] = out
+
+        def value(j):
+            a, low = slice(base + j * T, base + (j + 1) * T), j * T if own else 0
             dva[a, :] += mm(probs[h, a, low:ROWS], g[low:ROWS, cols])
-            dka[a, :] += mm(dsc[a, low:ROWS], q[low:ROWS, cols])
-
-    def dq_copy(part, k):
+
+        def key(j):
+            a, low = slice(base + j * T, base + (j + 1) * T), j * T if own else 0
+            c = slice(n * ROWS + j * T, n * ROWS + (j + 1) * T)
+            dka[a, :] += mm(dsc[c, low:ROWS], q[low:ROWS, cols])
+
+        first = [(grads, (i, j)) for i in range(NB) for j in range(i + 1 if own else NB)]
+        return first, [(value, (j,)) for j in range(NB)], [(key, (j,)) for j in range(NB)]
+
+    def blend(long, short):
+        taken = 0
+        for index, (unit, arg) in enumerate(long):
+            unit(*arg)
+            while taken < len(short) and taken * len(long) < (index + 1) * len(short):
+                short[taken][0](*short[taken][1])
+                taken += 1
+
+    def dq_copy(h, k):
         p = nxt(k)
         return send(
-            dq.at[ds(p * D, D), ds(part * WIDE, WIDE)],
-            dq_out.at[:, ds((hd * SPLIT + part) * WIDE, WIDE)],
-            d_s.at[part, k], d_r.at[part, k], dev(x, p),
-        )
-
-    def dq_local(part):
+            dq.at[ds(p * D, D), ds(h * D, D)], dq_out.at[:, ds((hd * GROUP + h) * D, D)], d_s.at[h, k], d_r.at[h, k], dev(x, p)
+        )
+
+    def dq_local(h):
         return pltpu.make_async_copy(
-            dq.at[ds(hd * D, D), ds(part * WIDE, WIDE)], dq_out.at[:, ds((hd * SPLIT + part) * WIDE, WIDE)], d_r.at[part, 0]
+            dq.at[ds(hd * D, D), ds(h * D, D)], dq_out.at[:, ds((hd * GROUP + h) * D, D)], d_r.at[h, 0]
+        )
+
+    def run(list_of_units):
+        for unit, arg in list_of_units:
+            unit(*arg)
+
+    def backward_half(heads, own):
+        if not own:
+            run(prepare(0, heads[0]))
+        pending = []
+        for n, h in enumerate(heads):
+            first, values, keys = units(n, h, own)
+            ahead = prepare(n + 1, heads[n + 1]) if not own and n + 1 < len(heads) else []
+            blend(first, ahead + values + pending)
+            pending = keys
+            if own:
+                dq_local(h).start()
+                for k in range(1, PEERS):
+                    dq_copy(h, k).start()
+        return pending
+
+    def out_copy(t, k, same):
+        src, dst = ((dkb, rk), (dvb, rv))[t]
+        p, slot = nxt(k), 1 if same else 0
+        return send(
+            src.at[ds(slot * ROWS + p * D, D), :], dst.at[slot, :, ds(hd * D, D)],
+            o_s.at[t, slot, k], o_r.at[t, slot, k], dev(x if same else 1 - x, p),
         )
 
     def backward_part(part, carry):
         wait_in(g_in, g, g_s, g_r, part)
-        lax.fori_loop(0, HEADS, lambda n, c: (backward(part * HEADS + n), c)[1], 0)
-        dq_local(part).start()
-        for k in range(1, PEERS):
-            dq_copy(part, k).start()
+        heads = [part * HEADS + n for n in range(HEADS)]
+        run(backward_half(heads, False))
+
+        @pl.when(jnp.logical_and(late, part == SPLIT - 1))
+        def _():
+            dkb[0:ROWS, :] = (dka[0:ROWS, :] * SCALE).astype(BF16)
+            dvb[0:ROWS, :] = dva[0:ROWS, :].astype(BF16)
+            for t in range(2):
+                for k in range(PEERS):
+                    out_copy(t, k, False).start()
+
+        run(backward_half(heads, True))
         return carry
 
     lax.fori_loop(0, SPLIT, backward_part, 0)
 
-    dkb[...] = (dka[...] * SCALE).astype(BF16)
-    dvb[...] = dva[...].astype(BF16)
-
-    def out_copy(t, k, same):
-        src, dst = ((dkb, rk), (dvb, rv))[t]
-        p = nxt(k)
-        base = ROWS if same else 0
-        slot = 1 if same else 0
-        index = k + (0 if same else PEERS)
-        return send(
-            src.at[ds(base + p * D, D), :], dst.at[slot, :, ds(hd * D, D)], o_s.at[t, index], o_r.at[t, index],
-            dev(x if same else 1 - x, p),
-        )
-
-    @pl.when(late)
-    def _():
-        for k in range(PEERS):
-            for t in range(2):
-                out_copy(t, k, False).start()
+    dkb[ROWS:KEYS, :] = (dka[ROWS:KEYS, :] * SCALE).astype(BF16)
+    dvb[ROWS:KEYS, :] = dva[ROWS:KEYS, :].astype(BF16)
 
     def out_local(t):
         src, dst = ((dkb, rk), (dvb, rv))[t]
@@ -374,7 +427,7 @@
         for t in range(2):
             for k in range(PEERS):
                 out_copy(t, k, False).wait_recv()
-            x_copy(t).wait_send()
+                x_copy(t, k).wait_send()
         dk_out[...] = (rk[0].astype(F32) + rk[1].astype(F32)).astype(BF16)
         dv_out[...] = (rv[0].astype(F32) + rv[1].astype(F32)).astype(BF16)
 
@@ -382,16 +435,21 @@
         for k in range(1, PEERS):
             kv_copy(k, t).wait_send()
     for part in range(SPLIT):
-        dq_local(part).wait()
         for k in range(1, PEERS):
             in_copy(q_in, q, q_s, q_r, part, k).wait_send()
             in_copy(g_in, g, g_s, g_r, part, k).wait_send()
-            dq_copy(part, k).wait()
+    for h in range(GROUP):
+        dq_local(h).wait()
+        for k in range(1, PEERS):
+            dq_copy(h, k).wait()
+
+
+def place(*refs):
+    for source, target in zip(refs[:4], refs[4:]):
+        target[...] = source[...]
 
 
 def body(queries, keys, values, cotangent, readout, rewards, saved, ends, segs):
-    place = lax.rem(lax.axis_index("dp"), PEERS)
-    heads = lax.dynamic_slice_in_dim(readout.reshape(PEERS * GROUP, D), place * GROUP, GROUP, 0).astype(F32)
     vmem = pl.BlockSpec(memory_space=pltpu.VMEM)
     hbm = pl.BlockSpec(memory_space=pl.ANY)
     dma = pltpu.SemaphoreType.DMA
@@ -432,26 +490,35 @@
             pltpu.VMEM((GROUP, PEERS, D), F32),
             pltpu.VMEM((GROUP, D, D), F32),
             pltpu.VMEM((D, D), F32),
-            pltpu.VMEM((8, ROWS), F32),
+            pltpu.VMEM((HEADS, 8, ROWS), F32),
             dma((SPLIT, PEERS)), dma((SPLIT, PEERS)),
             dma((SPLIT, PEERS)), dma((SPLIT, PEERS)),
-            dma((SPLIT, PEERS)), dma((SPLIT, PEERS)),
+            dma((GROUP, PEERS)), dma((GROUP, PEERS)),
             dma((2, PEERS)), dma((2, PEERS)),
-            dma((2,)), dma((2,)),
+            dma((2, PEERS)), dma((2, PEERS)),
             dma((16,)), dma((16,)),
             dma, dma,
             dma((PEERS,)), dma((PEERS,)),
-            dma((2, 2 * PEERS)), dma((2, 2 * PEERS)),
+            dma((2, 2, PEERS)), dma((2, 2, PEERS)),
             dma((2,)),
         ],
         compiler_params=pltpu.CompilerParams(
             collective_id=0, has_side_effects=True, vmem_limit_bytes=62 << 20
         ),
     )(
-        queries, keys, values, cotangent, heads,
+        queries, keys, values, cotangent, readout.reshape(1, PEERS * GROUP * D),
         rewards.reshape(1, D), saved.reshape(1, D), ends.reshape(1, D), segs.reshape(1, D),
     )
-    return (grads[0], grads[1], grads[2], grads[3].reshape(D))
+    blocks = [pl.BlockSpec((D // 4, a.shape[1]), lambda i: (i, 0)) for a in grads[:3]]
+    blocks.append(pl.BlockSpec((1, D), lambda i: (0, 0)))
+    done = pl.pallas_call(
+        place,
+        grid=(4,),
+        out_shape=[jax.ShapeDtypeStruct(a.shape, a.dtype) for a in grads],
+        in_specs=blocks,
+        out_specs=blocks,
+    )(*grads)
+    return (done[0], done[1], done[2], done[3].reshape(D))
 
 
 def solution(mesh):

time: 126 us -> 119 us (0.944)
  local copies, waits for them, and re-layouts: 5.08 us -> 1.35 us
  Pallas kernels: 119 us -> 116 us
  other arithmetic: 1.28 us -> 0 us
    pallas_call x1, Pallas kernels: 119 us -> 113 us  [body(): pl.pallas_call(kernel, out_shape=(jax.ShapeDtypeStruct(queries.shape, BF1...]
    unnamed x10 -> x0, local copies, waits for them, and re-layouts: 5.08 us -> none
    pallas_call x0 -> x1, Pallas kernels: none -> 3.95 us  [body(): pl.pallas_call(place, grid=(4,), out_shape=[jax.ShapeDtypeStruct(a.shape,...]
    reshape x0 -> x1, local copies, waits for them, and re-layouts: none -> 1.35 us  [body(): readout.reshape(1, PEERS * GROUP * D)]
    convert_element_type x1 -> x0, other arithmetic: 1.28 us -> none  [body(): lax.dynamic_slice_in_dim(readout.reshape(PEERS * GROUP, D), place * GROUP...]
where the time goes in v2:
time: 119 us
  Pallas kernels  116 us (97%)
  local copies, waits for them, and re-layouts  1.35 us (1%)
    pallas_call x1, Pallas kernels, body(): pl.pallas_call(kernel, out_shape=(jax.ShapeDtypeStruct(queries.shape, BF1...  113 us
    pallas_call x1, Pallas kernels, body(): pl.pallas_call(place, grid=(4,), out_shape=[jax.ShapeDtypeStruct(a.shape,...  3.95 us

profile of v2, /device:TPU:1, one launch (start us, length us, event | category | flops | bytes accessed | tf_op | source)
XLA Modules:
  0.0 118.5 jit_solution(12538069814903363166)
XLA Ops:
  0.6 1.4 %reshape.26.readout_in = bf16[1,8192]{1,0:T(2,128)(2,1)} reshape(bf16[8192]{0:T(1024)(128)(2,1)} %param.13) | data formatting | bytes 32768 | tf_op jit(solution)/shard_map/reshape | solution.py:509
  2.0 112.5 %shard_map.120 = (bf16[128,8192]{1,0:T(8,128)(2,1)}, bf16[128,1024]{1,0:T(8,128)(2,1)}, bf16[128,1024]{1,0:T(8,128)(2,1)}, f32[1,128]{1,0:T(1,128)}) custom-call(bf16[128,8192]{1,0:T(8,128)(2,1)} %q_in.1, bf16[128,1024]{1,0:T(8,128)(2,1)} %k_in.1, bf16[128,1024]{1,0:T(8,128)(2,1)} %v_in.1, bf16[128,8192]{1,0:T(8,128)(2,1)} %g_in.1, ...), custom_call_target="tpu_custom_call" | custom-call | tf_op jit(solution)/shard_map/pallas_call | solution.py:456
  114.5 3.9 %shard_map.121 = (bf16[128,8192]{1,0:T(8,128)(2,1)}, bf16[128,1024]{1,0:T(8,128)(2,1)}, bf16[128,1024]{1,0:T(8,128)(2,1)}, f32[1,128]{1,0:T(1,128)}) custom-call(bf16[128,8192]{1,0:T(8,128)(2,1)} %get-tuple-element.12.refs_0_, bf16[128,1024]{1,0:T(8,128)(2,1)} %get-tuple-element.13.refs_1_, bf16[128,1024]{1,0:T(8,128)(2,1)} %get-tuple-element.14.refs_2_, ...), custom_call_target="tpu_custom_call" | custom-call | tf_op jit(solution)/shard_map/pallas_call | solution.py:514

commit v3 on v2

--- a/solution.py
+++ b/solution.py
@@ -16,6 +16,7 @@
 KEYS = 2 * ROWS
 T = 256
 NB = ROWS // T
+STEP = 2
 SPLIT = 4
 HEADS = GROUP // SPLIT
 WIDE = HEADS * D
@@ -60,7 +61,7 @@
         )
 
     def readout_row(h):
-        return readout_in[:, ds((hd * GROUP + h) * D, D)].astype(F32)
+        return readout_in[:, ds((hd * GROUP + h) * D, D)]
 
     barrier = pltpu.get_barrier_semaphore()
     for k in range(1, 16):
@@ -140,16 +141,17 @@
     pl.semaphore_wait(barrier, 17)
     for k in range(1, 16):
         pk_copy(k).start()
-    for t in range(2):
-        kv_local(t).start()
-        for k in range(1, PEERS):
-            kv_copy(k, t).start()
-
     @pl.when(x == 0)
     def _():
         for t in range(2):
             for k in range(PEERS):
                 x_copy(t, k).start()
+
+    for t in range(2):
+        kv_local(t).start()
+        for k in range(1, PEERS):
+            kv_copy(k, t).start()
+
 
     for part in range(SPLIT):
         start_in(q_in, q, q_s, q_r, part)
@@ -209,27 +211,28 @@
         steps = [(h, i) for h in heads for i in range(NB)]
         state = {}
 
-        def score(t, j):
+        def score(t, j, to):
             h, i = steps[t]
             cols, r = ds(h * D, D), slice(i * T, (i + 1) * T)
             if j == 0:
                 state["q", t] = jnp.concatenate([q[r, cols], qm[r, :]], axis=1)
-            s = mm(kaug[j * T : (j + 1) * T, :], state["q", t], ((1,), (1,)))
-            if j == NB + i:
-                s = jnp.where(tile_sub <= tile_lane, s, -BIG)
-            sc[t % 2, j * T : (j + 1) * T, :] = s
-            part = jnp.max(s.reshape(T // 8, 8, T), axis=0)
+            s = mm(kaug[j * T : to * T, :], state["q", t], ((1,), (1,)))
+            if to == NB + i + 1:
+                own = jnp.where(tile_sub <= tile_lane, s[(to - 1 - j) * T :, :], -BIG)
+                s = own if to == j + 1 else jnp.concatenate([s[: (to - 1 - j) * T, :], own], axis=0)
+            sc[t % 2, j * T : to * T, :] = s
+            part = jnp.max(s.reshape((to - j) * T // 8, 8, T), axis=0)
             state["top", t] = part if j == 0 else jnp.maximum(state["top", t], part)
-            if j == NB + i:
+            if to == NB + i + 1:
                 state["top", t] = jnp.max(state["top", t], axis=0, keepdims=True) * EXP2
 
-        def weigh(t, j):
+        def weigh(t, j, to):
             h, i = steps[t]
             r = slice(i * T, (i + 1) * T)
-            p = jnp.exp2(sc[t % 2, j * T : (j + 1) * T, :] * EXP2 - state["top", t])
-            part = jnp.sum(p.reshape(T // 8, 8, T), axis=0)
+            p = jnp.exp2(sc[t % 2, j * T : to * T, :] * EXP2 - state["top", t])
+            part = jnp.sum(p.reshape((to - j) * T // 8, 8, T), axis=0)
             state["sum", t] = part if j == 0 else state["sum", t] + part
-            probs[h, j * T : (j + 1) * T, r] = p.astype(BF16)
+            probs[h, j * T : to * T, r] = p.astype(BF16)
 
         def output(t):
             h, i = steps[t]
@@ -248,11 +251,11 @@
         for t in range(len(steps) + 2):
             if t >= 2:
                 output(t - 2)
-            for j in range(2 * NB):
+            for j in range(0, 2 * NB, STEP):
                 if t < len(steps) and j <= NB + steps[t][1]:
-                    score(t, j)
+                    score(t, j, min(j + STEP, NB + steps[t][1] + 1))
                 if 1 <= t <= len(steps) and j <= NB + steps[t - 1][1]:
-                    weigh(t - 1, j)
+                    weigh(t - 1, j, min(j + STEP, NB + steps[t - 1][1] + 1))
 
     def forward_part(part, carry):
         wait_in(q_in, q, q_s, q_r, part)
@@ -308,13 +311,13 @@
         cols = ds(h * D, D)
         base = ROWS if own else 0
 
-        def grads(i, j):
-            r, a = slice(i * T, (i + 1) * T), slice(base + j * T, base + (j + 1) * T)
-            c = slice(n * ROWS + j * T, n * ROWS + (j + 1) * T)
+        def grads(i, j, to):
+            r, a = slice(i * T, (i + 1) * T), slice(base + j * T, base + to * T)
+            c = slice(n * ROWS + j * T, n * ROWS + to * T)
             dp = mm(v[a, :], g[r, cols], ((1,), (1,)))
             dsc[c, r] = (probs[h, a, r].astype(F32) * (dp - rd[n, 0:1, r])).astype(BF16)
             count = i + 1 if own else NB
-            if j == count - 1:
+            if to == count:
                 out = mm(kt[:, base : base + count * T], dsc[n * ROWS : n * ROWS + count * T, r])
                 keep = slice(i * D, (i + 1) * D)
                 if own:
@@ -331,7 +334,11 @@
             c = slice(n * ROWS + j * T, n * ROWS + (j + 1) * T)
             dka[a, :] += mm(dsc[c, low:ROWS], q[low:ROWS, cols])
 
-        first = [(grads, (i, j)) for i in range(NB) for j in range(i + 1 if own else NB)]
+        first = [
+            (grads, (i, j, min(j + STEP, count)))
+            for i, count in enumerate(range(1, NB + 1) if own else [NB] * NB)
+            for j in range(0, count, STEP)
+        ]
         return first, [(value, (j,)) for j in range(NB)], [(key, (j,)) for j in range(NB)]
 
     def blend(long, short):
@@ -506,7 +513,7 @@
             collective_id=0, has_side_effects=True, vmem_limit_bytes=62 << 20
         ),
     )(
-        queries, keys, values, cotangent, readout.reshape(1, PEERS * GROUP * D),
+        queries, keys, values, cotangent, readout.astype(F32).reshape(1, PEERS * GROUP * D),
         rewards.reshape(1, D), saved.reshape(1, D), ends.reshape(1, D), segs.reshape(1, D),
     )
     blocks = [pl.BlockSpec((D // 4, a.shape[1]), lambda i: (i, 0)) for a in grads[:3]]

time: 119 us -> 118 us (level)
  local copies, waits for them, and re-layouts: 1.35 us -> 0 us
  other arithmetic: 0 us -> 1.34 us
    reshape x1 -> x0, local copies, waits for them, and re-layouts: 1.35 us -> none  [body(): readout.reshape(1, PEERS * GROUP * D)]
    reshape x0 -> x1, other arithmetic: none -> 1.34 us  [body(): readout.astype(F32).reshape(1, PEERS * GROUP * D)]
where the time goes in v3:
time: 118 us
  Pallas kernels  116 us (98%)
  other arithmetic  1.34 us (1%)
    pallas_call x1, Pallas kernels, body(): pl.pallas_call(kernel, out_shape=(jax.ShapeDtypeStruct(queries.shape, BF1...  112 us
    pallas_call x1, Pallas kernels, body(): pl.pallas_call(place, grid=(4,), out_shape=[jax.ShapeDtypeStruct(a.shape,...  3.95 us

profile of v3, /device:TPU:1, one launch (start us, length us, event | category | flops | bytes accessed | tf_op | source)
XLA Modules:
  0.0 118.1 jit_solution(8620493388980799928)
XLA Ops:
  0.6 1.3 %reshape.35 = f32[8192]{0:T(1024)} convert(bf16[8192]{0:T(1024)(128)(2,1)} %param.13) | non-fusion elementwise | flops 8192 | bytes 49152 | tf_op jit(solution)/shard_map/reshape | solution.py:516
  2.0 112.0 %shard_map.120 = (bf16[128,8192]{1,0:T(8,128)(2,1)}, bf16[128,1024]{1,0:T(8,128)(2,1)}, bf16[128,1024]{1,0:T(8,128)(2,1)}, f32[1,128]{1,0:T(1,128)}) custom-call(bf16[128,8192]{1,0:T(8,128)(2,1)} %q_in.1, bf16[128,1024]{1,0:T(8,128)(2,1)} %k_in.1, bf16[128,1024]{1,0:T(8,128)(2,1)} %v_in.1, bf16[128,8192]{1,0:T(8,128)(2,1)} %g_in.1, f32[1,8192]{1,0:T(1,128)} %bitcast.6, ...), custom_call_target="tpu_custom_call" | custom-call | tf_op jit(solution)/shard_map/pallas_call | solution.py:463
  114.0 3.9 %shard_map.121 = (bf16[128,8192]{1,0:T(8,128)(2,1)}, bf16[128,1024]{1,0:T(8,128)(2,1)}, bf16[128,1024]{1,0:T(8,128)(2,1)}, f32[1,128]{1,0:T(1,128)}) custom-call(bf16[128,8192]{1,0:T(8,128)(2,1)} %get-tuple-element.12.refs_0_, bf16[128,1024]{1,0:T(8,128)(2,1)} %get-tuple-element.13.refs_1_, bf16[128,1024]{1,0:T(8,128)(2,1)} %get-tuple-element.14.refs_2_, ...), custom_call_target="tpu_custom_call" | custom-call | tf_op jit(solution)/shard_map/pallas_call | solution.py:521

commit v4 on v3

--- a/solution.py
+++ b/solution.py
@@ -17,7 +17,7 @@
 T = 256
 NB = ROWS // T
 STEP = 2
-SPLIT = 4
+SPLIT = 8
 HEADS = GROUP // SPLIT
 WIDE = HEADS * D
 BIG = 1e30
@@ -260,9 +260,9 @@
     def forward_part(part, carry):
         wait_in(q_in, q, q_s, q_r, part)
 
-        @pl.when(part >= 2)
+        @pl.when(part >= SPLIT // 2)
         def _():
-            start_in(g_in, g, g_s, g_r, part - 2)
+            start_in(g_in, g, g_s, g_r, part - SPLIT // 2)
 
         forward([part * HEADS + n for n in range(HEADS)])
         return carry
@@ -281,7 +281,7 @@
 
     for k in range(1, PEERS):
         es_copy(k).start()
-    for part in range(SPLIT - 2, SPLIT):
+    for part in range(SPLIT // 2, SPLIT):
         start_in(g_in, g, g_s, g_r, part)
     for b in range(2 * PEERS):
         kt[:, b * D : (b + 1) * D] = kaug[b * D : (b + 1) * D, 0:D].T
@@ -516,11 +516,11 @@
         queries, keys, values, cotangent, readout.astype(F32).reshape(1, PEERS * GROUP * D),
         rewards.reshape(1, D), saved.reshape(1, D), ends.reshape(1, D), segs.reshape(1, D),
     )
-    blocks = [pl.BlockSpec((D // 4, a.shape[1]), lambda i: (i, 0)) for a in grads[:3]]
+    blocks = [pl.BlockSpec((D // 2, a.shape[1]), lambda i: (i, 0)) for a in grads[:3]]
     blocks.append(pl.BlockSpec((1, D), lambda i: (0, 0)))
     done = pl.pallas_call(
         place,
-        grid=(4,),
+        grid=(2,),
         out_shape=[jax.ShapeDtypeStruct(a.shape, a.dtype) for a in grads],
         in_specs=blocks,
         out_specs=blocks,

time: 118 us -> 121 us (1.025)
  Pallas kernels: 116 us -> 118 us
    pallas_call x1, Pallas kernels: 112 us -> 115 us  [body(): pl.pallas_call(kernel, out_shape=(jax.ShapeDtypeStruct(queries.shape, BF1...]
where the time goes in v4:
time: 121 us; the launch traced here: 120 us
  Pallas kernels  118 us (98%)
  other arithmetic  1.34 us (1%)
    pallas_call x1, Pallas kernels, body(): pl.pallas_call(kernel, out_shape=(jax.ShapeDtypeStruct(queries.shape, BF1...  115 us
    pallas_call x1, Pallas kernels, body(): pl.pallas_call(place, grid=(2,), out_shape=[jax.ShapeDtypeStruct(a.shape,...  2.88 us

profile of v4, /device:TPU:1, one launch (start us, length us, event | category | flops | bytes accessed | tf_op | source)
XLA Modules:
  0.0 120.3 jit_solution(4649097136007870023)
XLA Ops:
  0.6 1.3 %reshape.35 = f32[8192]{0:T(1024)} convert(bf16[8192]{0:T(1024)(128)(2,1)} %param.13) | non-fusion elementwise | flops 8192 | bytes 49152 | tf_op jit(solution)/shard_map/reshape | solution.py:516
  2.0 115.4 %shard_map.120 = (bf16[128,8192]{1,0:T(8,128)(2,1)}, bf16[128,1024]{1,0:T(8,128)(2,1)}, bf16[128,1024]{1,0:T(8,128)(2,1)}, f32[1,128]{1,0:T(1,128)}) custom-call(bf16[128,8192]{1,0:T(8,128)(2,1)} %q_in.1, bf16[128,1024]{1,0:T(8,128)(2,1)} %k_in.1, bf16[128,1024]{1,0:T(8,128)(2,1)} %v_in.1, bf16[128,8192]{1,0:T(8,128)(2,1)} %g_in.1, f32[1,8192]{1,0:T(1,128)} %bitcast.6, ...), custom_call_target="tpu_custom_call" | custom-call | tf_op jit(solution)/shard_map/pallas_call | solution.py:463
  117.4 2.9 %shard_map.121 = (bf16[128,8192]{1,0:T(8,128)(2,1)}, bf16[128,1024]{1,0:T(8,128)(2,1)}, bf16[128,1024]{1,0:T(8,128)(2,1)}, f32[1,128]{1,0:T(1,128)}) custom-call(bf16[128,8192]{1,0:T(8,128)(2,1)} %get-tuple-element.12.refs_0_, bf16[128,1024]{1,0:T(8,128)(2,1)} %get-tuple-element.13.refs_1_, bf16[128,1024]{1,0:T(8,128)(2,1)} %get-tuple-element.14.refs_2_, ...), custom_call_target="tpu_custom_call" | custom-call | tf_op jit(solution)/shard_map/pallas_call | solution.py:521
